TPU v7x, 512 devices: a whole 4x4x16 slice. The times are simulated.
512 devices in a mesh: seq: 32 (over x, z_lo), expert: 8 (over z_hi, y), mp: 2 (over core).
Axes of the slice: x: 4, y: 4, z: 16 (z_hi: 2, z_lo: 8; z = z_hi * 8 + z_lo), core: 2. Of those that a mesh axis runs over, the one named last changes fastest.
Arguments:
- queries: bfloat16 [8, 32, 128, 4096], P('expert', 'seq', None, 'mp'), may hold values from -6 to 6
- out_grad: bfloat16 [8, 32, 128, 4096], P('expert', 'seq', None, 'mp'), may hold values from -6 to 6
- prompt_kv: bfloat16 [8, 1024, 2, 256], P('expert', 'seq', None, 'mp'), may hold values from -6 to 6
- resp_kv: bfloat16 [8, 32, 128, 2, 256], P('expert', 'seq', None, None, 'mp'), may hold values from -6 to 6
- lengths: int32 [8, 32], P('expert', 'seq'), may hold values from 1 to 128, 3072 in all within a row
- grads: bfloat16 [8, 32, 128, 2048], P('expert', 'seq'), may hold values from -6 to 6
- routes: int32 [8, 32, 128, 8], P('expert', 'seq'), may hold values from 0 to 127, all different within a row; in each aligned block of 128 rows (0 to 127, 128 to 255, ..., all dimensions but the last counted through in order) at most 16 rows name the same one
- gates: float32 [8, 32, 128, 8], P('expert', 'seq'), may hold values from 0.1 to 1
- down_weight: bfloat16 [8, 1536, 2048], P('expert', 'mp'), may hold values from -0.125 to 0.125
Outputs:
- prompt_dkv: float32 [8, 1024, 2, 256], P('expert', 'seq', None, 'mp')
- resp_dkv: float32 [8, 32, 128, 2, 256], P('expert', 'seq', None, None, 'mp')
- expert_grad: bfloat16 [32, 8, 8, 16, 1536], P('seq', None, 'expert', None, 'mp')
Inputs may be any that keep to these rules, and one draw needn't show every extreme that they name: `routes`: the 8 experts of a token differ; among the rows of one device no expert is named by more than 16 rows.
All inputs are finite; a program needn't handle non-finite values. No bound on the sum of `lengths` on one device may be relied on, other than what follows from the above.
Results may differ from a plain program's by a relative error of at most 0.0049.
Values may be sent and summed in bfloat16 or wider, within the bound.
A program may use at most 64 MiB of HBM per device.

v0:
```python
import jax
import jax.numpy as jnp
from jax import lax
from jax.sharding import PartitionSpec as P

HD = 128


def local(queries, out_grad, prompt_kv, resp_kv, lengths, grads, routes, gates, down_weight):
    query_rows = queries[0, 0]
    row_count = query_rows.shape[0]
    kv_heads = resp_kv.shape[-1] // HD
    q_heads = query_rows.shape[-1] // HD
    group_size = q_heads // kv_heads
    score_scale = HD ** (-0.5)
    query_heads = query_rows.reshape(row_count, kv_heads, group_size, HD)
    gathered = lax.all_gather(prompt_kv, "seq", axis=1, tiled=True)
    prompt_len = gathered.shape[1]
    key_rows = jnp.concatenate([gathered[0, :, 0], resp_kv[0, 0, :, 0]], 0).reshape(
        -1, kv_heads, HD
    )
    value_rows = jnp.concatenate([gathered[0, :, 1], resp_kv[0, 0, :, 1]], 0).reshape(
        -1, kv_heads, HD
    )
    key_total = key_rows.shape[0]
    length = lengths[0, 0]
    position = jnp.arange(row_count)
    allowed = jnp.concatenate(
        [jnp.ones((row_count, prompt_len), jnp.bool_), position[None, :] <= position[:, None]], 1
    )
    scores = (
        jnp.einsum("icgd,jcd->cgij", query_heads, key_rows, preferred_element_type=jnp.float32)
        * score_scale
    )
    scores = jnp.where(allowed, scores, -jnp.inf)
    numerators = jnp.exp(scores - jnp.max(scores, -1, keepdims=True))
    attention = numerators / jnp.sum(numerators, -1, keepdims=True)
    attention_low = attention.astype(jnp.bfloat16)
    grad_out = out_grad[0, 0]
    grad_rows = jnp.where((position < length)[:, None], grad_out, jnp.zeros_like(grad_out))
    grad_heads = grad_rows.reshape(row_count, kv_heads, group_size, HD)
    grad_probs = jnp.einsum(
        "icgd,jcd->cgij", grad_heads, value_rows, preferred_element_type=jnp.float32
    )
    row_delta = jnp.sum(attention * grad_probs, -1, keepdims=True)
    grad_low = (attention * (grad_probs - row_delta) * score_scale).astype(jnp.bfloat16)
    grad_keys = jnp.einsum(
        "cgij,icgd->jcd", grad_low, query_heads, preferred_element_type=jnp.float32
    )
    grad_values = jnp.einsum(
        "cgij,icgd->jcd", attention_low, grad_heads, preferred_element_type=jnp.float32
    )
    every_term = jnp.stack(
        [
            grad_keys.reshape(key_total, kv_heads * HD),
            grad_values.reshape(key_total, kv_heads * HD),
        ],
        1,
    )
    prompt_part = lax.psum_scatter(every_term[:prompt_len], "seq", scatter_dimension=0, tiled=True)
    own_part = every_term[prompt_len:]
    token_rows = grads[0, 0]
    route_ids = routes[0, 0]
    gate_rows = gates[0, 0]
    local_experts = down_weight.shape[0]
    expert_devices = lax.axis_size("expert")
    capacity = row_count // 8
    expert_ids = jnp.arange(local_experts * expert_devices)
    matches = route_ids[:, :, None] == expert_ids[None, None, :]
    named_rows = jnp.any(matches, 1)
    valid_rows = (position < length).astype(jnp.float32)
    route_weight = (
        jnp.sum(jnp.where(matches, gate_rows[:, :, None], jnp.zeros_like(gate_rows[:, :, None])), 1)
        * valid_rows[:, None]
    )
    slot_index = jnp.cumsum(named_rows.astype(jnp.int32), 0) - 1
    selection = named_rows[:, :, None] & (
        slot_index[:, :, None] == jnp.arange(capacity)[None, None, :]
    )
    picked = jnp.einsum(
        "ixc,id->xcd",
        selection.astype(jnp.bfloat16),
        token_rows,
        preferred_element_type=jnp.float32,
    )
    slot_gate = jnp.einsum(
        "ixc,ix->xc", selection.astype(jnp.float32), route_weight, precision=lax.Precision.HIGHEST
    )
    outgoing = (
        (picked * slot_gate[:, :, None])
        .astype(jnp.bfloat16)
        .reshape(expert_devices, local_experts, capacity, token_rows.shape[1])
    )
    expert_grad = jnp.einsum(
        "sxcd,xfd->sxcf",
        lax.all_to_all(outgoing, "expert", split_axis=0, concat_axis=0, tiled=True),
        down_weight,
        preferred_element_type=jnp.float32,
    ).astype(jnp.bfloat16)
    return (prompt_part[None], own_part[None, None], expert_grad[None])


def solution(mesh):
    placed = (
        P("expert", "seq", None, "mp"),
        P("expert", "seq", None, "mp"),
        P("expert", "seq", None, "mp"),
        P("expert", "seq", None, None, "mp"),
        P("expert", "seq"),
        P("expert", "seq", None, None),
        P("expert", "seq", None, None),
        P("expert", "seq", None, None),
        P("expert", "mp", None),
    )
    return jax.shard_map(
        local,
        mesh=mesh,
        in_specs=placed,
        out_specs=(
            P("expert", "seq", None, "mp"),
            P("expert", "seq", None, None, "mp"),
            P("seq", None, "expert", None, "mp"),
        ),
        check_vma=False,
    )
```

profile of v0, /device:TPU:8, one launch (start us, length us, event | category | flops | bytes accessed | tf_op | source)
XLA Modules:
  0.0 430.9 jit_solution(1173876097495905706)
XLA Ops:
  7.2 0.0 copy-start
  8.0 0.5 iota_compare_fusion.3
  8.5 0.7 fusion.49
  9.2 0.1 copy.54
  9.3 0.2 reduce_window_sum.11
  9.5 0.7 select_reduce_fusion
  10.3 0.2 fusion.44
  10.5 2.1 fusion.21
  12.6 18.2 %all-to-all-start = ((bf16[8,1,16,2048]{3,2,1,0:T(8,128)(2,1)}), bf16[8,1,16,2048]{3,2,1,0:T(8,128)(2,1)}, u32[]{:S(2)}, u32[]{:S(2)}) async-start(bf16[8,1,16,2048]{3,2,1,0:T(8,128)(2,1)} %fusion.21), calls=%async_computation.1 | async-start | bytes 1048576 | tf_op jit(solution)/shard_map/all_to_all | solution.py:96
  30.8 0.0 reduce-scatter.2.cloned.1.call-start
  30.8 1.0 fusion.59
  31.8 0.7 copy.45
  32.5 134.5 %all_gather.3 = bf16[1,1024,2,128]{3,1,2,0:T(8,128)(2,1)S(1)} all-gather(bf16[1,32,2,128]{3,1,2,0:T(8,128)(2,1)S(1)} %copy.45), channel_id=1, replica_groups=mesh['seq'=32,'expert'=8,'mp'=2] {'seq'}, dimensions={1}, use_global_device_ids=true | all-gather | bytes 540672 | tf_op jit(solution)/shard_map/all_gather | solution.py:17
  167.0 0.7 slice_bitcast_fusion.1
  167.8 1.9 copy.68
  169.7 2.0 copy.64
  171.7 1.1 select_bitcast_fusion
  172.9 0.1 copy.69
  173.1 0.0 copy-start.4
  173.1 0.0 copy-start.6
  173.1 2.5 fusion.60
  175.6 1.2 fusion.5
  176.9 0.0 copy-done.4
  176.9 0.0 copy-done.6
  176.9 0.0 copy-start.5
  176.9 1.6 fusion.17
  178.5 0.0 copy-start.2
  178.5 0.0 copy-done.5
  178.5 0.0 copy-start.1
  178.5 2.2 fusion
  180.8 0.0 copy-done.1
  180.8 2.7 fusion.14
  183.5 0.0 copy-done.2
  183.5 0.0 copy-start.3
  183.5 0.8 copy-done.3
  184.3 1.1 fusion.28
  185.4 0.0 reduce-scatter.2.cloned.1.call-update
  185.4 0.9 fusion.42
  186.3 0.8 copy.58
  187.0 0.0 all-to-all-done
  187.0 0.0 copy-done
  187.0 2.9 fusion.25
  189.9 232.7 %reduce-scatter.2.cloned.1.call-done = f32[32,2,128]{2,0,1:T(8,128)} async-done(((f32[1024,2,128]{2,0,1:T(8,128)}), f32[32,2,128]{2,0,1:T(8,128)}) %reduce-scatter.2.cloned.1.call-update) | async-done | bytes 32784 | tf_op jit(solution)/shard_map/reduce_scatter | solution.py:60
  422.7 1.4 copy.57
  (7 shorter events, 0.1 us)
Async XLA Ops:
  7.2 179.9 %copy-start = (bf16[1,768,2048]{2,1,0:T(8,128)(2,1)S(1)}, bf16[1,768,2048]{2,1,0:T(8,128)(2,1)}, u32[]{:S(2)}) copy-start(bf16[1,768,2048]{2,1,0:T(8,128)(2,1)} %param.17) | copy-start | bytes 9437188
  12.6 174.4 %all-to-all-start = ((bf16[8,1,16,2048]{3,2,1,0:T(8,128)(2,1)}), bf16[8,1,16,2048]{3,2,1,0:T(8,128)(2,1)}, u32[]{:S(2)}, u32[]{:S(2)}) async-start(bf16[8,1,16,2048]{3,2,1,0:T(8,128)(2,1)} %fusion.21), calls=%async_computation.1 | async-start | bytes 1048576 | tf_op jit(solution)/shard_map/all_to_all | solution.py:96
  30.8 391.9 %reduce-scatter.2.cloned.1.call-start = ((), (), s32[]{:S(2)}) async-start(), calls=%async_computation.2 | async-start | bytes 1081344 | tf_op jit(solution)/shard_map/reduce_scatter | solution.py:60
  173.1 3.8 copy-start.4
  173.1 3.8 copy-start.6
  176.9 1.6 copy-start.5
  178.5 5.0 %copy-start.2 = (f32[1152,1,128]{2,0,1:T(8,128)}, f32[1152,1,128]{2,0,1:T(8,128)S(1)}, u32[]{:S(2)}) copy-start(f32[1152,1,128]{2,0,1:T(8,128)S(1)} %fusion.17) | copy-start | bytes 1769476
  178.5 2.3 copy-start.1
  183.5 0.8 copy-start.3
Sparse Core Ops, SparseCore 0:
  185.5 237.1 reduce-scatter.1
where the time goes:
time: 432 us; the launch traced here: 431 us
  waiting for transfers between devices  233 us (54%)
  blocking collectives  134 us (31%)
  starting transfers between devices  18.2 us (4%)
  between operations  15 us (3%)
  matrix products  14.2 us (3%)
  local copies, waits for them, and re-layouts  9.8 us (2%)
  other arithmetic  6.48 us (2%)
    reduce_scatter x1, waiting for transfers between devices, local(): lax.psum_scatter(every_term[:prompt_len], 'seq', scatter_dimension=0, til...  233 us
    all_gather x1, blocking collectives, local(): gathered = lax.all_gather(prompt_kv, 'seq', axis=1, tiled=True)  134 us
    all_to_all x1, starting transfers between devices, local(): lax.all_to_all(outgoing, 'expert', split_axis=0, concat_axis=0, tiled=True)  18.2 us
  transfers between devices with their start and end apart: 2, of which 1 were waited for; matrix products, arithmetic and copies ran while one was open for 5% of the time, Pallas kernels for 0%

commit v1 on v0

--- a/solution.py
+++ b/solution.py
@@ -4,6 +4,15 @@
 from jax.sharding import PartitionSpec as P
 
 HD = 128
+trace_fields = lambda target: jnp.concatenate(
+    jax.lax.all_to_all(
+        jnp.stack([target for _ in range(jax.lax.axis_size("seq"))]),
+        axis_name="seq",
+        split_axis=0,
+        concat_axis=0,
+    ),
+    1,
+)
 
 
 def local(queries, out_grad, prompt_kv, resp_kv, lengths, grads, routes, gates, down_weight):
@@ -14,7 +23,7 @@
     group_size = q_heads // kv_heads
     score_scale = HD ** (-0.5)
     query_heads = query_rows.reshape(row_count, kv_heads, group_size, HD)
-    gathered = lax.all_gather(prompt_kv, "seq", axis=1, tiled=True)
+    gathered = trace_fields(prompt_kv)
     prompt_len = gathered.shape[1]
     key_rows = jnp.concatenate([gathered[0, :, 0], resp_kv[0, 0, :, 0]], 0).reshape(
         -1, kv_heads, HD

time: 432 us -> 328 us (0.76)
  blocking collectives: 134 us -> 0 us
  waiting for transfers between devices: 233 us -> 254 us
  starting transfers between devices: 18.2 us -> 26.2 us
    all_gather x1 -> x0, blocking collectives: 134 us -> none  [local(): gathered = lax.all_gather(prompt_kv, 'seq', axis=1, tiled=True)]
    all_to_all x0 -> x1, waiting for transfers between devices: none -> 18.2 us  [jax.lax.all_to_all(jnp.stack([target for _ in range(jax.lax.axis_size('se...]
    all_to_all x0 -> x1, starting transfers between devices: none -> 15.5 us  [jax.lax.all_to_all(jnp.stack([target for _ in range(jax.lax.axis_size('se...]
    all_to_all x1, waiting for transfers between devices: 0.01 us -> 9.4 us  [local(): lax.all_to_all(outgoing, 'expert', split_axis=0, concat_axis=0, tiled=True)]
    all_to_all x1, starting transfers between devices: 18.2 us -> 10.7 us  [local(): lax.all_to_all(outgoing, 'expert', split_axis=0, concat_axis=0, tiled=True)]
    reduce_scatter x1, waiting for transfers between devices: 233 us -> 227 us  [local(): lax.psum_scatter(every_term[:prompt_len], 'seq', scatter_dimension=0, til...]
  transfers between devices with their start and end apart: 2 -> 3, of which waited for: 1 -> 3; matrix products, arithmetic and copies ran while one was open for 5% -> 9% of each run, Pallas kernels for 0% -> 0%
where the time goes in v1:
time: 328 us; the launch traced here: 327 us
  waiting for transfers between devices  254 us (77%)
  starting transfers between devices  26.2 us (8%)
  between operations  14.9 us (5%)
  matrix products  14 us (4%)
  local copies, waits for them, and re-layouts  12 us (4%)
  other arithmetic  5.96 us (2%)
    reduce_scatter x1, waiting for transfers between devices, local(): lax.psum_scatter(every_term[:prompt_len], 'seq', scatter_dimension=0, til...  227 us
    all_to_all x1, waiting for transfers between devices, jax.lax.all_to_all(jnp.stack([target for _ in range(jax.lax.axis_size('se...  18.2 us
    all_to_all x1, starting transfers between devices, jax.lax.all_to_all(jnp.stack([target for _ in range(jax.lax.axis_size('se...  15.5 us
    all_to_all x1, starting transfers between devices, local(): lax.all_to_all(outgoing, 'expert', split_axis=0, concat_axis=0, tiled=True)  10.7 us
    all_to_all x1, waiting for transfers between devices, local(): lax.all_to_all(outgoing, 'expert', split_axis=0, concat_axis=0, tiled=True)  9.4 us
  transfers between devices with their start and end apart: 3, of which 3 were waited for; matrix products, arithmetic and copies ran while one was open for 9% of the time, Pallas kernels for 0%

profile of v1, /device:TPU:8, one launch (start us, length us, event | category | flops | bytes accessed | tf_op | source)
XLA Modules:
  0.0 327.4 jit_solution(1892655159648154)
XLA Ops:
  7.2 0.0 copy-start
  7.2 0.9 copy.46
  8.1 0.9 stack.4
  9.0 15.5 %all-to-all-start = ((bf16[32,1,32,2,128]{4,2,3,1,0:T(8,128)(2,1)}), bf16[32,1,32,2,128]{4,2,3,1,0:T(8,128)(2,1)}, u32[]{:S(2)}, u32[]{:S(2)}) async-start(bf16[32,1,32,2,128]{4,2,3,1,0:T(8,128)(2,1)} %stack.4), calls=%async_computation | async-start | bytes 1048576 | tf_op jit(solution)/shard_map/all_to_all | solution.py:8
  24.5 1.9 copy.70
  27.1 2.0 copy.66
  29.1 1.1 select_bitcast_fusion
  30.3 0.9 copy.71
  31.2 0.7 fusion.49
  31.9 0.1 copy.56
  32.0 0.2 reduce_window_sum.11
  32.3 0.7 select_reduce_fusion
  33.0 0.2 fusion.44
  33.2 2.1 fusion.21
  35.3 1.0 fusion.59
  36.4 18.2 %all-to-all-done = bf16[32,1,32,2,128]{4,2,3,1,0:T(8,128)(2,1)} async-done(((bf16[32,1,32,2,128]{4,2,3,1,0:T(8,128)(2,1)}), bf16[32,1,32,2,128]{4,2,3,1,0:T(8,128)(2,1)}, u32[]{:S(2)}, u32[]{:S(2)}) %all-to-all-start) | async-done | bytes 524320 | tf_op jit(solution)/shard_map/all_to_all | solution.py:8
  54.7 10.7 %all-to-all-start.1 = ((bf16[8,1,16,2048]{3,2,1,0:T(8,128)(2,1)}), bf16[8,1,16,2048]{3,2,1,0:T(8,128)(2,1)}, u32[]{:S(2)}, u32[]{:S(2)}) async-start(bf16[8,1,16,2048]{3,2,1,0:T(8,128)(2,1)} %fusion.21), calls=%async_computation.2 | async-start | bytes 1048576 | tf_op jit(solution)/shard_map/all_to_all | solution.py:105
  65.3 0.0 reduce-scatter.2.cloned.1.call-start
  65.3 1.1 copy.47
  66.4 0.0 copy-start.5
  66.5 2.5 fusion.60
  69.0 1.2 fusion.5
  70.2 0.0 copy-done.5
  70.2 0.0 copy-start.1
  70.3 2.1 fusion
  72.3 0.0 copy-done.1
  72.3 0.0 copy-start.4
  72.4 2.6 fusion.14
  74.9 0.0 copy-start.2
  74.9 0.0 copy-done.4
  75.0 1.6 fusion.17
  76.5 0.0 copy-done.2
  76.6 0.0 copy-start.3
  76.6 0.8 copy-done.3
  77.4 1.1 fusion.28
  78.4 0.0 reduce-scatter.2.cloned.1.call-update
  78.5 9.4 %all-to-all-done.1 = bf16[8,1,16,2048]{3,2,1,0:T(8,128)(2,1)} async-done(((bf16[8,1,16,2048]{3,2,1,0:T(8,128)(2,1)}), bf16[8,1,16,2048]{3,2,1,0:T(8,128)(2,1)}, u32[]{:S(2)}, u32[]{:S(2)}) %all-to-all-start.1) | async-done | bytes 524320 | tf_op jit(solution)/shard_map/all_to_all | solution.py:105
  87.9 0.0 copy-done
  87.9 2.9 fusion.25
  90.8 0.9 fusion.42
  91.7 0.8 copy.60
  92.4 226.7 %reduce-scatter.2.cloned.1.call-done = f32[32,2,128]{2,0,1:T(8,128)} async-done(((f32[1024,2,128]{2,0,1:T(8,128)}), f32[32,2,128]{2,0,1:T(8,128)}) %reduce-scatter.2.cloned.1.call-update) | async-done | bytes 32784 | tf_op jit(solution)/shard_map/reduce_scatter | solution.py:69
  319.1 1.4 copy.59
  (9 shorter events, 0.2 us)
Async XLA Ops:
  7.2 80.7 %copy-start = (bf16[1,768,2048]{2,1,0:T(8,128)(2,1)S(1)}, bf16[1,768,2048]{2,1,0:T(8,128)(2,1)}, u32[]{:S(2)}) copy-start(bf16[1,768,2048]{2,1,0:T(8,128)(2,1)} %param.17) | copy-start | bytes 9437188
  9.0 45.7 %all-to-all-start = ((bf16[32,1,32,2,128]{4,2,3,1,0:T(8,128)(2,1)}), bf16[32,1,32,2,128]{4,2,3,1,0:T(8,128)(2,1)}, u32[]{:S(2)}, u32[]{:S(2)}) async-start(bf16[32,1,32,2,128]{4,2,3,1,0:T(8,128)(2,1)} %stack.4), calls=%async_computation | async-start | bytes 1048576 | tf_op jit(solution)/shard_map/all_to_all | solution.py:8
  54.7 33.2 %all-to-all-start.1 = ((bf16[8,1,16,2048]{3,2,1,0:T(8,128)(2,1)}), bf16[8,1,16,2048]{3,2,1,0:T(8,128)(2,1)}, u32[]{:S(2)}, u32[]{:S(2)}) async-start(bf16[8,1,16,2048]{3,2,1,0:T(8,128)(2,1)} %fusion.21), calls=%async_computation.2 | async-start | bytes 1048576 | tf_op jit(solution)/shard_map/all_to_all | solution.py:105
  65.3 253.8 %reduce-scatter.2.cloned.1.call-start = ((), (), s32[]{:S(2)}) async-start(), calls=%async_computation.3 | async-start | bytes 1081344 | tf_op jit(solution)/shard_map/reduce_scatter | solution.py:69
  66.4 3.8 %copy-start.5 = (bf16[16,8,16,128]{3,2,1,0:T(8,128)(2,1)S(1)}, bf16[16,8,16,128]{3,2,1,0:T(8,128)(2,1)}, u32[]{:S(2)}) copy-start(bf16[16,8,16,128]{3,2,1,0:T(8,128)(2,1)} %copy.71) | copy-start | bytes 1572868
  70.2 2.1 copy-start.1
  72.3 2.6 copy-start.4
  74.9 1.6 copy-start.2
  76.6 0.8 copy-start.3
Sparse Core Ops, SparseCore 0:
  78.6 240.4 reduce-scatter.1
